TPU v7x, 512 devices: a whole 4x8x8 slice. The times are simulated.
512 devices in a mesh: ctx: 32 (over z, y_hi, core), tp: 16 (over x, y_lo).
Axes of the slice: x: 4, y: 8 (y_hi: 2, y_lo: 4; y = y_hi * 4 + y_lo), z: 8, core: 2. Of those that a mesh axis runs over, the one named last changes fastest.
Arguments:
- q_proj: bfloat16 [4096, 4096], P('ctx', 'tp'), may hold values from -6 to 6
- k_proj: bfloat16 [4096, 4096], P('ctx', 'tp'), may hold values from -6 to 6
- v_proj: bfloat16 [4096, 4096], P('ctx', 'tp'), may hold values from -6 to 6
- saved_conv: bfloat16 [4096, 4096], P('ctx', 'tp'), may hold values from -6 to 6
- out_grad: bfloat16 [4096, 4096], P('ctx', 'tp'), may hold values from -6 to 6
- out_weight: bfloat16 [4096, 4096], P('tp'), may hold values from -0.09375 to 0.09375
- filter_taps: bfloat16 [4096, 4096], P('ctx', 'tp'), may hold values from -1.1 to 1.1
Outputs:
- dq_grad: bfloat16 [4096, 4096], P('ctx', 'tp')
- dk_grad: bfloat16 [4096, 4096], P('ctx', 'tp')
- dv_grad: bfloat16 [4096, 4096], P('ctx', 'tp')
- filter_grad: float32 [4096, 4096], P('ctx', 'tp')
All inputs are finite; a program needn't handle non-finite values.
Results may differ from a plain program's by a relative error of at most 0.003.
Values may be sent and summed in bfloat16 or wider, within the bound.
A program may use at most 128 MiB of HBM per device.

v0:
```python
import math

import jax
import jax.numpy as jnp
from jax import lax
from jax.sharding import PartitionSpec as P


def from_behind(value, axis, steps):
    count = lax.axis_size(axis)
    pairs = [(source, (source + steps) % count) for source in range(count)]
    return lax.ppermute(value, axis, pairs)


def passed_along(block, axis, distance):
    devices = range(lax.axis_size(axis))
    route = [(i - distance, i) for i in devices if i - distance in devices]
    return lax.ppermute(block, axis, route)


def matmul(left, right):
    return jnp.dot(left, right, precision=lax.Precision.HIGHEST, preferred_element_type=jnp.float32)


def split_table(table):
    upper = lax.optimization_barrier(table.astype(jnp.bfloat16))
    lower = (table - upper.astype(jnp.float32)).astype(jnp.bfloat16)
    return (upper, lower)


def half_matmul(table, signal):
    upper, lower = split_table(table)
    return jnp.dot(upper, signal, preferred_element_type=jnp.float32) + jnp.dot(
        lower, signal, preferred_element_type=jnp.float32
    )


def make_tables(rows):
    index = jnp.arange(rows, dtype=jnp.int32)
    long_index = jnp.arange(2 * rows, dtype=jnp.int32)
    angle = (index[:, None] * index[None, :] % (2 * rows)).astype(jnp.float32) * (math.pi / rows)
    angle_back = (long_index[:, None] * index[None, :] % (2 * rows)).astype(jnp.float32) * (
        math.pi / rows
    )
    weight = jnp.where(index == 0, 1.0, 2.0).astype(jnp.float32) / (2.0 * rows)
    alternate = (1 - 2 * (index % 2)).astype(jnp.float32)
    alternate_back = (1 - 2 * (long_index % 2)).astype(jnp.float32) / (2.0 * rows)
    return (
        jnp.cos(angle),
        -jnp.sin(angle),
        alternate,
        jnp.cos(angle_back) * weight[None, :],
        -jnp.sin(angle_back) * weight[None, :],
        alternate_back,
    )


def forward(signal, tables):
    fwd_cos, fwd_sin, alternate = (tables[0], tables[1], tables[2])
    return (matmul(fwd_cos, signal), matmul(fwd_sin, signal), matmul(alternate[None, :], signal))


def forward_half(signal, tables):
    fwd_cos, fwd_sin, alternate = (tables[0], tables[1], tables[2])
    signs = alternate[None, :].astype(jnp.bfloat16)
    return (
        half_matmul(fwd_cos, signal),
        half_matmul(fwd_sin, signal),
        jnp.dot(signs, signal, preferred_element_type=jnp.float32),
    )


def inverse(spectrum, tables, count):
    inv_cos, inv_sin, alternate_back = (tables[3], tables[4], tables[5])
    return (
        matmul(inv_cos[:count], spectrum[0])
        + matmul(inv_sin[:count], spectrum[1])
        + alternate_back[:count, None] * spectrum[2]
    )


def correlate(first, second):
    real_part = first[0] * second[0] + first[1] * second[1]
    imag_part = first[0] * second[1] - first[1] * second[0]
    return (real_part, imag_part, first[2] * second[2])


def add_lags(filter_terms, lagged, step, active, rows):
    later = jnp.asarray(step >= 1, jnp.float32)
    filter_terms = filter_terms.at[step].add(lagged[:rows] * active)
    return filter_terms.at[jnp.maximum(step - 1, 0)].add(lagged[rows:] * (active * later))


def body(q_proj, k_proj, v_proj, saved_conv, out_grad, out_weight, filter_taps):
    rows = q_proj.shape[0]
    chans = q_proj.shape[1]
    blocks = lax.axis_size("ctx")
    me_index = lax.axis_index("ctx")
    tables = make_tables(rows)
    empty = jnp.zeros((rows, chans), jnp.float32)
    d_gated = lax.dot_general(
        lax.all_gather(out_grad, "tp", axis=1, tiled=True),
        out_weight,
        (((1,), (1,)), ((), ())),
        preferred_element_type=jnp.float32,
    )
    dq_grad = (d_gated * saved_conv.astype(jnp.float32)).astype(jnp.bfloat16)
    dz_local = d_gated * q_proj.astype(jnp.float32)
    gated = (k_proj.astype(jnp.float32) * v_proj.astype(jnp.float32)).astype(jnp.bfloat16)
    whole_filter = lax.all_gather(filter_taps, "ctx", axis=0, tiled=True)
    filter_blocks = whole_filter.reshape(blocks, rows, chans)
    cos_upper, cos_lower = split_table(tables[0])
    sin_upper, sin_lower = split_table(tables[1])
    spec_real = jnp.einsum(
        "fn,bnc->bfc", cos_upper, filter_blocks, preferred_element_type=jnp.float32
    ) + jnp.einsum("fn,bnc->bfc", cos_lower, filter_blocks, preferred_element_type=jnp.float32)
    spec_imag = jnp.einsum(
        "fn,bnc->bfc", sin_upper, filter_blocks, preferred_element_type=jnp.float32
    ) + jnp.einsum("fn,bnc->bfc", sin_lower, filter_blocks, preferred_element_type=jnp.float32)
    spec_top = jnp.einsum(
        "n,bnc->bc",
        tables[2].astype(jnp.bfloat16),
        filter_blocks,
        preferred_element_type=jnp.float32,
    )[:, None, :]
    parity = tables[2][:, None]

    def lag_spectrum(step):
        earlier = jnp.maximum(step - 1, 0)
        keep = jnp.asarray(step >= 1, jnp.float32)
        pieces = []
        for stack, factor in ((spec_real, parity), (spec_imag, parity), (spec_top, 1.0)):
            current = lax.dynamic_index_in_dim(stack, step, 0, keepdims=False)
            before = lax.dynamic_index_in_dim(stack, earlier, 0, keepdims=False)
            pieces.append(current + keep * factor * before)
        return (pieces[0], pieces[1], pieces[2])

    filter_terms = jnp.zeros((blocks, rows, chans), jnp.float32)
    dz_spec = forward(dz_local, tables)

    def carried_step(step, state):
        partial_value, moving, terms = state
        active = jnp.asarray(me_index >= step, jnp.float32)
        partial_value = partial_value + active * inverse(
            correlate(lag_spectrum(step), dz_spec), tables, rows
        )
        moving_spec = forward_half(moving, tables)
        lagged = inverse(correlate(moving_spec, dz_spec), tables, 2 * rows)
        terms = add_lags(terms, lagged, step, active, rows)
        partial_value = from_behind(partial_value, "ctx", 1)
        moving = passed_along(moving, "ctx", 1)
        return (partial_value, moving, terms)

    du_local, moving_last, filter_terms = lax.fori_loop(
        0, blocks, carried_step, (empty, gated, filter_terms)
    )
    summed = lax.psum_scatter(
        filter_terms.reshape(blocks * rows, chans), "ctx", scatter_dimension=0, tiled=True
    )
    filter_grad = summed * float(rows * blocks) ** (-0.5)
    dk_grad = (du_local * v_proj.astype(jnp.float32)).astype(jnp.bfloat16)
    dv_grad = (du_local * k_proj.astype(jnp.float32)).astype(jnp.bfloat16)
    return (dq_grad, dk_grad, dv_grad, filter_grad)


def solution(mesh):
    in_specs = (
        P("ctx", "tp"),
        P("ctx", "tp"),
        P("ctx", "tp"),
        P("ctx", "tp"),
        P("ctx", "tp"),
        P("tp", None),
        P("ctx", "tp"),
    )
    out_specs = (P("ctx", "tp"), P("ctx", "tp"), P("ctx", "tp"), P("ctx", "tp"))
    return jax.shard_map(body, mesh=mesh, in_specs=in_specs, out_specs=out_specs, check_vma=False)
```

profile of v0, /device:TPU:1, one launch (start us, length us, event | category | flops | bytes accessed | tf_op | source)
XLA Modules:
  0.0 921.8 jit_solution(6137578330895444131)
XLA Ops:
  10.7 69.9 %all-gather.3.cloned.1.call-done = bf16[128,4096]{1,0:T(8,128)(2,1)} async-done(((bf16[128,256]{1,0:T(8,128)(2,1)}), bf16[128,4096]{1,0:T(8,128)(2,1)}) %all-gather.3.cloned.1.call-update) | async-done | bytes 1048592 | tf_op jit(solution)/shard_map/all_gather | solution.py:102
  85.4 97.2 %all-gather.5.cloned.1.call-done = bf16[4096,256]{1,0:T(8,128)(2,1)} async-done(((bf16[128,256]{1,0:T(8,128)(2,1)}), bf16[4096,256]{1,0:T(8,128)(2,1)}) %all-gather.5.cloned.1.call-update) | async-done | bytes 2097168 | tf_op jit(solution)/shard_map/all_gather | solution.py:110
  196.0 568.7 %while.23 = (s32[]{:T(128)}, f32[128,256]{0,1:T(8,128)S(1)}, bf16[128,256]{1,0:T(8,128)(2,1)S(1)}, f32[32,128,256]{1,2,0:T(8,128)}, s32[]{:T(128)}, /*index=5*/f...) while((s32[]{:T(128)}, f32[128,256]{0,1:T(8,128)S(1)}, ...), condition=%wide.region_3.4_spmd.clone.clone, body=%wide.region_0.3_spmd.clone.clone.sunk | while | flops 337464864 | bytes 7294348 | solution.py:154
  210.9 8.4 collective-permute-start.1
  248.4 5.4 collective-permute-start.1
  282.8 7.4 collective-permute-start.1
  319.3 6.0 collective-permute-start.1
  338.1 5.1 collective-permute-start.1
  355.6 5.3 collective-permute-start.1
  373.7 5.1 collective-permute-start.1
  391.2 5.2 collective-permute-start.1
  409.2 5.0 collective-permute-start.1
  426.7 6.0 collective-permute-start.1
  445.4 5.1 collective-permute-start.1
  463.1 5.1 collective-permute-start.1
  480.6 5.0 collective-permute-start.1
  498.1 5.1 collective-permute-start.1
  516.1 5.1 collective-permute-start.1
  533.7 5.1 collective-permute-start.1
  551.3 5.1 collective-permute-start.1
  568.8 5.1 collective-permute-start.1
  587.1 5.0 collective-permute-start.1
  604.6 5.1 collective-permute-start.1
  622.1 5.1 collective-permute-start.1
  639.7 5.1 collective-permute-start.1
  657.8 5.0 collective-permute-start.1
  675.3 5.1 collective-permute-start.1
  710.7 5.1 collective-permute-start.1
  729.5 5.2 collective-permute-start.1
  747.2 5.1 collective-permute-start.1
  764.7 5.6 copy.13
  771.9 141.8 %reduce-scatter.2.cloned.1.call-done = f32[128,256]{1,0:T(8,128)} async-done(((f32[4096,256]{1,0:T(8,128)}), f32[128,256]{1,0:T(8,128)}) %reduce-scatter.2.cloned.1.call-update) | async-done | bytes 131088 | tf_op jit(solution)/shard_map/reduce_scatter | solution.py:157
  (685 shorter events, 445.3 us)
Async XLA Ops:
  7.2 73.4 %all-gather.3.cloned.1.call-start = ((), (), s32[]{:S(2)}) async-start(), calls=%async_computation.1 | async-start | bytes 1114112 | tf_op jit(solution)/shard_map/all_gather | solution.py:102
  7.9 174.7 %all-gather.5.cloned.1.call-start = ((), (), s32[]{:S(2)}) async-start(), calls=%async_computation.2 | async-start | bytes 2162688 | tf_op jit(solution)/shard_map/all_gather | solution.py:110
  8.7 905.0 %reduce-scatter.2.cloned.1.call-start = ((), (), s32[]{:S(2)}) async-start(), calls=%async_computation.3 | async-start | bytes 4325376 | tf_op jit(solution)/shard_map/reduce_scatter | solution.py:157
  210.9 21.1 %collective-permute-start.1 = (bf16[128,256]{1,0:T(8,128)(2,1)S(1)}, bf16[128,256]{1,0:T(8,128)(2,1)S(1)}, u32[]{:S(2)}, u32[]{:S(2)}) collective-permute-start(bf16[128,256]{1,0:T(8,128)(2,1)S(1)} %copy.25), channel_id=1, source_target_pairs={{0,16},{16,32},{32,48},{48,64},{64,80},{80,96},{96,112},{112,128},... | collective-permute-start | bytes 196616 | tf_op jit(solution)/shard_map/while/body/eval_jaxpr/ppermute | solution.py:18
  232.0 16.4 %collective-permute-start.1 = (bf16[128,256]{1,0:T(8,128)(2,1)S(1)}, bf16[128,256]{1,0:T(8,128)(2,1)S(1)}, u32[]{:S(2)}, u32[]{:S(2)}) collective-permute-start(bf16[128,256]{1,0:T(8,128)(2,1)S(1)} %copy.25), channel_id=1, source_target_pairs={{0,16},{16,32},{32,48},{48,64},{64,80},{80,96},{96,112},{112,128},... | collective-permute-start | bytes 196616 | tf_op jit(solution)/shard_map/while/body/eval_jaxpr/ppermute | solution.py:18
  248.4 18.1 %collective-permute-start.1 = (bf16[128,256]{1,0:T(8,128)(2,1)S(1)}, bf16[128,256]{1,0:T(8,128)(2,1)S(1)}, u32[]{:S(2)}, u32[]{:S(2)}) collective-permute-start(bf16[128,256]{1,0:T(8,128)(2,1)S(1)} %copy.25), channel_id=1, source_target_pairs={{0,16},{16,32},{32,48},{48,64},{64,80},{80,96},{96,112},{112,128},... | collective-permute-start | bytes 196616 | tf_op jit(solution)/shard_map/while/body/eval_jaxpr/ppermute | solution.py:18
  282.8 20.1 %collective-permute-start.1 = (bf16[128,256]{1,0:T(8,128)(2,1)S(1)}, bf16[128,256]{1,0:T(8,128)(2,1)S(1)}, u32[]{:S(2)}, u32[]{:S(2)}) collective-permute-start(bf16[128,256]{1,0:T(8,128)(2,1)S(1)} %copy.25), channel_id=1, source_target_pairs={{0,16},{16,32},{32,48},{48,64},{64,80},{80,96},{96,112},{112,128},... | collective-permute-start | bytes 196616 | tf_op jit(solution)/shard_map/while/body/eval_jaxpr/ppermute | solution.py:18
  319.3 18.7 %collective-permute-start.1 = (bf16[128,256]{1,0:T(8,128)(2,1)S(1)}, bf16[128,256]{1,0:T(8,128)(2,1)S(1)}, u32[]{:S(2)}, u32[]{:S(2)}) collective-permute-start(bf16[128,256]{1,0:T(8,128)(2,1)S(1)} %copy.25), channel_id=1, source_target_pairs={{0,16},{16,32},{32,48},{48,64},{64,80},{80,96},{96,112},{112,128},... | collective-permute-start | bytes 196616 | tf_op jit(solution)/shard_map/while/body/eval_jaxpr/ppermute | solution.py:18
  338.1 17.5 %collective-permute-start.1 = (bf16[128,256]{1,0:T(8,128)(2,1)S(1)}, bf16[128,256]{1,0:T(8,128)(2,1)S(1)}, u32[]{:S(2)}, u32[]{:S(2)}) collective-permute-start(bf16[128,256]{1,0:T(8,128)(2,1)S(1)} %copy.25), channel_id=1, source_target_pairs={{0,16},{16,32},{32,48},{48,64},{64,80},{80,96},{96,112},{112,128},... | collective-permute-start | bytes 196616 | tf_op jit(solution)/shard_map/while/body/eval_jaxpr/ppermute | solution.py:18
  355.6 18.1 %collective-permute-start.1 = (bf16[128,256]{1,0:T(8,128)(2,1)S(1)}, bf16[128,256]{1,0:T(8,128)(2,1)S(1)}, u32[]{:S(2)}, u32[]{:S(2)}) collective-permute-start(bf16[128,256]{1,0:T(8,128)(2,1)S(1)} %copy.25), channel_id=1, source_target_pairs={{0,16},{16,32},{32,48},{48,64},{64,80},{80,96},{96,112},{112,128},... | collective-permute-start | bytes 196616 | tf_op jit(solution)/shard_map/while/body/eval_jaxpr/ppermute | solution.py:18
  373.7 17.5 %collective-permute-start.1 = (bf16[128,256]{1,0:T(8,128)(2,1)S(1)}, bf16[128,256]{1,0:T(8,128)(2,1)S(1)}, u32[]{:S(2)}, u32[]{:S(2)}) collective-permute-start(bf16[128,256]{1,0:T(8,128)(2,1)S(1)} %copy.25), channel_id=1, source_target_pairs={{0,16},{16,32},{32,48},{48,64},{64,80},{80,96},{96,112},{112,128},... | collective-permute-start | bytes 196616 | tf_op jit(solution)/shard_map/while/body/eval_jaxpr/ppermute | solution.py:18
  391.2 17.9 %collective-permute-start.1 = (bf16[128,256]{1,0:T(8,128)(2,1)S(1)}, bf16[128,256]{1,0:T(8,128)(2,1)S(1)}, u32[]{:S(2)}, u32[]{:S(2)}) collective-permute-start(bf16[128,256]{1,0:T(8,128)(2,1)S(1)} %copy.25), channel_id=1, source_target_pairs={{0,16},{16,32},{32,48},{48,64},{64,80},{80,96},{96,112},{112,128},... | collective-permute-start | bytes 196616 | tf_op jit(solution)/shard_map/while/body/eval_jaxpr/ppermute | solution.py:18
  409.2 17.5 %collective-permute-start.1 = (bf16[128,256]{1,0:T(8,128)(2,1)S(1)}, bf16[128,256]{1,0:T(8,128)(2,1)S(1)}, u32[]{:S(2)}, u32[]{:S(2)}) collective-permute-start(bf16[128,256]{1,0:T(8,128)(2,1)S(1)} %copy.25), channel_id=1, source_target_pairs={{0,16},{16,32},{32,48},{48,64},{64,80},{80,96},{96,112},{112,128},... | collective-permute-start | bytes 196616 | tf_op jit(solution)/shard_map/while/body/eval_jaxpr/ppermute | solution.py:18
  426.7 18.7 %collective-permute-start.1 = (bf16[128,256]{1,0:T(8,128)(2,1)S(1)}, bf16[128,256]{1,0:T(8,128)(2,1)S(1)}, u32[]{:S(2)}, u32[]{:S(2)}) collective-permute-start(bf16[128,256]{1,0:T(8,128)(2,1)S(1)} %copy.25), channel_id=1, source_target_pairs={{0,16},{16,32},{32,48},{48,64},{64,80},{80,96},{96,112},{112,128},... | collective-permute-start | bytes 196616 | tf_op jit(solution)/shard_map/while/body/eval_jaxpr/ppermute | solution.py:18
  445.4 17.6 %collective-permute-start.1 = (bf16[128,256]{1,0:T(8,128)(2,1)S(1)}, bf16[128,256]{1,0:T(8,128)(2,1)S(1)}, u32[]{:S(2)}, u32[]{:S(2)}) collective-permute-start(bf16[128,256]{1,0:T(8,128)(2,1)S(1)} %copy.25), channel_id=1, source_target_pairs={{0,16},{16,32},{32,48},{48,64},{64,80},{80,96},{96,112},{112,128},... | collective-permute-start | bytes 196616 | tf_op jit(solution)/shard_map/while/body/eval_jaxpr/ppermute | solution.py:18
  463.1 17.5 %collective-permute-start.1 = (bf16[128,256]{1,0:T(8,128)(2,1)S(1)}, bf16[128,256]{1,0:T(8,128)(2,1)S(1)}, u32[]{:S(2)}, u32[]{:S(2)}) collective-permute-start(bf16[128,256]{1,0:T(8,128)(2,1)S(1)} %copy.25), channel_id=1, source_target_pairs={{0,16},{16,32},{32,48},{48,64},{64,80},{80,96},{96,112},{112,128},... | collective-permute-start | bytes 196616 | tf_op jit(solution)/shard_map/while/body/eval_jaxpr/ppermute | solution.py:18
  480.6 17.5 %collective-permute-start.1 = (bf16[128,256]{1,0:T(8,128)(2,1)S(1)}, bf16[128,256]{1,0:T(8,128)(2,1)S(1)}, u32[]{:S(2)}, u32[]{:S(2)}) collective-permute-start(bf16[128,256]{1,0:T(8,128)(2,1)S(1)} %copy.25), channel_id=1, source_target_pairs={{0,16},{16,32},{32,48},{48,64},{64,80},{80,96},{96,112},{112,128},... | collective-permute-start | bytes 196616 | tf_op jit(solution)/shard_map/while/body/eval_jaxpr/ppermute | solution.py:18
  498.1 18.0 %collective-permute-start.1 = (bf16[128,256]{1,0:T(8,128)(2,1)S(1)}, bf16[128,256]{1,0:T(8,128)(2,1)S(1)}, u32[]{:S(2)}, u32[]{:S(2)}) collective-permute-start(bf16[128,256]{1,0:T(8,128)(2,1)S(1)} %copy.25), channel_id=1, source_target_pairs={{0,16},{16,32},{32,48},{48,64},{64,80},{80,96},{96,112},{112,128},... | collective-permute-start | bytes 196616 | tf_op jit(solution)/shard_map/while/body/eval_jaxpr/ppermute | solution.py:18
  516.1 17.6 %collective-permute-start.1 = (bf16[128,256]{1,0:T(8,128)(2,1)S(1)}, bf16[128,256]{1,0:T(8,128)(2,1)S(1)}, u32[]{:S(2)}, u32[]{:S(2)}) collective-permute-start(bf16[128,256]{1,0:T(8,128)(2,1)S(1)} %copy.25), channel_id=1, source_target_pairs={{0,16},{16,32},{32,48},{48,64},{64,80},{80,96},{96,112},{112,128},... | collective-permute-start | bytes 196616 | tf_op jit(solution)/shard_map/while/body/eval_jaxpr/ppermute | solution.py:18
  533.7 17.5 %collective-permute-start.1 = (bf16[128,256]{1,0:T(8,128)(2,1)S(1)}, bf16[128,256]{1,0:T(8,128)(2,1)S(1)}, u32[]{:S(2)}, u32[]{:S(2)}) collective-permute-start(bf16[128,256]{1,0:T(8,128)(2,1)S(1)} %copy.25), channel_id=1, source_target_pairs={{0,16},{16,32},{32,48},{48,64},{64,80},{80,96},{96,112},{112,128},... | collective-permute-start | bytes 196616 | tf_op jit(solution)/shard_map/while/body/eval_jaxpr/ppermute | solution.py:18
  551.3 17.6 %collective-permute-start.1 = (bf16[128,256]{1,0:T(8,128)(2,1)S(1)}, bf16[128,256]{1,0:T(8,128)(2,1)S(1)}, u32[]{:S(2)}, u32[]{:S(2)}) collective-permute-start(bf16[128,256]{1,0:T(8,128)(2,1)S(1)} %copy.25), channel_id=1, source_target_pairs={{0,16},{16,32},{32,48},{48,64},{64,80},{80,96},{96,112},{112,128},... | collective-permute-start | bytes 196616 | tf_op jit(solution)/shard_map/while/body/eval_jaxpr/ppermute | solution.py:18
  568.8 18.2 %collective-permute-start.1 = (bf16[128,256]{1,0:T(8,128)(2,1)S(1)}, bf16[128,256]{1,0:T(8,128)(2,1)S(1)}, u32[]{:S(2)}, u32[]{:S(2)}) collective-permute-start(bf16[128,256]{1,0:T(8,128)(2,1)S(1)} %copy.25), channel_id=1, source_target_pairs={{0,16},{16,32},{32,48},{48,64},{64,80},{80,96},{96,112},{112,128},... | collective-permute-start | bytes 196616 | tf_op jit(solution)/shard_map/while/body/eval_jaxpr/ppermute | solution.py:18
  587.1 17.5 %collective-permute-start.1 = (bf16[128,256]{1,0:T(8,128)(2,1)S(1)}, bf16[128,256]{1,0:T(8,128)(2,1)S(1)}, u32[]{:S(2)}, u32[]{:S(2)}) collective-permute-start(bf16[128,256]{1,0:T(8,128)(2,1)S(1)} %copy.25), channel_id=1, source_target_pairs={{0,16},{16,32},{32,48},{48,64},{64,80},{80,96},{96,112},{112,128},... | collective-permute-start | bytes 196616 | tf_op jit(solution)/shard_map/while/body/eval_jaxpr/ppermute | solution.py:18
  604.6 17.6 %collective-permute-start.1 = (bf16[128,256]{1,0:T(8,128)(2,1)S(1)}, bf16[128,256]{1,0:T(8,128)(2,1)S(1)}, u32[]{:S(2)}, u32[]{:S(2)}) collective-permute-start(bf16[128,256]{1,0:T(8,128)(2,1)S(1)} %copy.25), channel_id=1, source_target_pairs={{0,16},{16,32},{32,48},{48,64},{64,80},{80,96},{96,112},{112,128},... | collective-permute-start | bytes 196616 | tf_op jit(solution)/shard_map/while/body/eval_jaxpr/ppermute | solution.py:18
  622.1 17.5 %collective-permute-start.1 = (bf16[128,256]{1,0:T(8,128)(2,1)S(1)}, bf16[128,256]{1,0:T(8,128)(2,1)S(1)}, u32[]{:S(2)}, u32[]{:S(2)}) collective-permute-start(bf16[128,256]{1,0:T(8,128)(2,1)S(1)} %copy.25), channel_id=1, source_target_pairs={{0,16},{16,32},{32,48},{48,64},{64,80},{80,96},{96,112},{112,128},... | collective-permute-start | bytes 196616 | tf_op jit(solution)/shard_map/while/body/eval_jaxpr/ppermute | solution.py:18
  639.7 18.1 %collective-permute-start.1 = (bf16[128,256]{1,0:T(8,128)(2,1)S(1)}, bf16[128,256]{1,0:T(8,128)(2,1)S(1)}, u32[]{:S(2)}, u32[]{:S(2)}) collective-permute-start(bf16[128,256]{1,0:T(8,128)(2,1)S(1)} %copy.25), channel_id=1, source_target_pairs={{0,16},{16,32},{32,48},{48,64},{64,80},{80,96},{96,112},{112,128},... | collective-permute-start | bytes 196616 | tf_op jit(solution)/shard_map/while/body/eval_jaxpr/ppermute | solution.py:18
  657.8 17.5 %collective-permute-start.1 = (bf16[128,256]{1,0:T(8,128)(2,1)S(1)}, bf16[128,256]{1,0:T(8,128)(2,1)S(1)}, u32[]{:S(2)}, u32[]{:S(2)}) collective-permute-start(bf16[128,256]{1,0:T(8,128)(2,1)S(1)} %copy.25), channel_id=1, source_target_pairs={{0,16},{16,32},{32,48},{48,64},{64,80},{80,96},{96,112},{112,128},... | collective-permute-start | bytes 196616 | tf_op jit(solution)/shard_map/while/body/eval_jaxpr/ppermute | solution.py:18
  675.3 17.9 %collective-permute-start.1 = (bf16[128,256]{1,0:T(8,128)(2,1)S(1)}, bf16[128,256]{1,0:T(8,128)(2,1)S(1)}, u32[]{:S(2)}, u32[]{:S(2)}) collective-permute-start(bf16[128,256]{1,0:T(8,128)(2,1)S(1)} %copy.25), channel_id=1, source_target_pairs={{0,16},{16,32},{32,48},{48,64},{64,80},{80,96},{96,112},{112,128},... | collective-permute-start | bytes 196616 | tf_op jit(solution)/shard_map/while/body/eval_jaxpr/ppermute | solution.py:18
  693.2 17.5 %collective-permute-start.1 = (bf16[128,256]{1,0:T(8,128)(2,1)S(1)}, bf16[128,256]{1,0:T(8,128)(2,1)S(1)}, u32[]{:S(2)}, u32[]{:S(2)}) collective-permute-start(bf16[128,256]{1,0:T(8,128)(2,1)S(1)} %copy.25), channel_id=1, source_target_pairs={{0,16},{16,32},{32,48},{48,64},{64,80},{80,96},{96,112},{112,128},... | collective-permute-start | bytes 196616 | tf_op jit(solution)/shard_map/while/body/eval_jaxpr/ppermute | solution.py:18
  710.7 18.8 %collective-permute-start.1 = (bf16[128,256]{1,0:T(8,128)(2,1)S(1)}, bf16[128,256]{1,0:T(8,128)(2,1)S(1)}, u32[]{:S(2)}, u32[]{:S(2)}) collective-permute-start(bf16[128,256]{1,0:T(8,128)(2,1)S(1)} %copy.25), channel_id=1, source_target_pairs={{0,16},{16,32},{32,48},{48,64},{64,80},{80,96},{96,112},{112,128},... | collective-permute-start | bytes 196616 | tf_op jit(solution)/shard_map/while/body/eval_jaxpr/ppermute | solution.py:18
  729.5 17.6 %collective-permute-start.1 = (bf16[128,256]{1,0:T(8,128)(2,1)S(1)}, bf16[128,256]{1,0:T(8,128)(2,1)S(1)}, u32[]{:S(2)}, u32[]{:S(2)}) collective-permute-start(bf16[128,256]{1,0:T(8,128)(2,1)S(1)} %copy.25), channel_id=1, source_target_pairs={{0,16},{16,32},{32,48},{48,64},{64,80},{80,96},{96,112},{112,128},... | collective-permute-start | bytes 196616 | tf_op jit(solution)/shard_map/while/body/eval_jaxpr/ppermute | solution.py:18
  747.2 17.5 %collective-permute-start.1 = (bf16[128,256]{1,0:T(8,128)(2,1)S(1)}, bf16[128,256]{1,0:T(8,128)(2,1)S(1)}, u32[]{:S(2)}, u32[]{:S(2)}) collective-permute-start(bf16[128,256]{1,0:T(8,128)(2,1)S(1)} %copy.25), channel_id=1, source_target_pairs={{0,16},{16,32},{32,48},{48,64},{64,80},{80,96},{96,112},{112,128},... | collective-permute-start | bytes 196616 | tf_op jit(solution)/shard_map/while/body/eval_jaxpr/ppermute | solution.py:18
  (41 other events, 505.1 us)
Sparse Core Ops, SparseCore 0:
  10.0 70.5 all-gather.2
  84.0 98.5 all-gather.4
  770.5 143.1 reduce-scatter.1
where the time goes:
time: 931 us; the launch traced here: 922 us
  waiting for transfers between devices  310 us (33%)
  starting transfers between devices  231 us (25%)
  matrix products  181 us (19%)
  other arithmetic  173 us (19%)
  between operations  13.8 us (1%)
    ppermute x32, starting transfers between devices, passed_along(): return lax.ppermute(block, axis, route)  164 us
    reduce_scatter x1, waiting for transfers between devices, body(): lax.psum_scatter(filter_terms.reshape(blocks * rows, chans), 'ctx', scatt...  142 us
    dot_general x131, matrix products, matmul(): jnp.dot(left, right, precision=lax.Precision.HIGHEST, preferred_element_t...  129 us
    all_gather x1, waiting for transfers between devices, body(): whole_filter = lax.all_gather(filter_taps, 'ctx', axis=0, tiled=True)  97.2 us
    scatter-add x32, other arithmetic, add_lags(): filter_terms = filter_terms.at[step].add(lagged[:rows] * active)  72.8 us
    scatter-add x32, other arithmetic, add_lags(): filter_terms.at[jnp.maximum(step - 1, 0)]  70 us
    all_gather x1, waiting for transfers between devices, body(): lax.all_gather(out_grad, 'tp', axis=1, tiled=True)  69.9 us
    ppermute x32, starting transfers between devices, from_behind(): return lax.ppermute(value, axis, pairs)  66.9 us
  transfers between devices with their start and end apart: 67, of which 3 were waited for; matrix products, arithmetic and copies ran while one was open for 37% of the time, Pallas kernels for 0%

commit v1 on v0

v1 whole, which is shorter than its diff:
```python
import functools
import math

import jax
import jax.numpy as jnp
import ml_dtypes
import numpy as np
from jax import lax
from jax.experimental import pallas as pl
from jax.experimental.pallas import tpu as pltpu
from jax.sharding import PartitionSpec as P

MESH = pl.DeviceIdType.MESH
F32 = jnp.float32
BF16 = jnp.bfloat16
XN = 4
YN = 4
GROUP = 8


def halves(table):
    upper = table.astype(ml_dtypes.bfloat16)
    lower = (table - upper.astype(np.float64)).astype(ml_dtypes.bfloat16)
    return np.concatenate([upper, lower], axis=1)


def make_tables(block):
    n = np.arange(block)
    turns = np.outer(n, 2 * n + 1) % (4 * block)
    angle = turns * (math.pi / (2 * block))
    forward = np.concatenate([np.cos(angle), -np.sin(angle)], axis=1)
    back = np.concatenate([np.cos(angle).T, -np.sin(angle).T], axis=0) / block
    return halves(forward), halves(back)


def split(value):
    upper = value.astype(BF16)
    return upper, (value - upper.astype(F32)).astype(BF16)


def mm(left, right):
    return jnp.dot(left, right, preferred_element_type=F32)


def fused(
    nctx, f_hbm, k_hbm, v_hbm, q_hbm, og_hbm, s_hbm, w_hbm, fwd_hbm, inv_hbm,
    dq_ref, dk_ref, dv_ref, fg_ref,
    f_ref, k_ref, v_ref, q_ref, og_ref, s_ref, w, fwd, inv, og_all, acc, qt, fgs, xf, zs, zin, xspec, zt, obuf, rs, ret,
    local_sem, send_ag, recv_y, recv_x, recv_r, send_f, recv_f, send_z, recv_z, send_o, recv_o,
):
    rows, chans = q_ref.shape
    nb = nctx // 2
    block = 2 * rows
    half = rows // 2
    me_c = lax.axis_index("ctx")
    me_t = lax.axis_index("tp")
    x = lax.div(me_t, YN)
    y = lax.rem(me_t, YN)
    right = lax.rem(x + 1, XN)
    left = lax.rem(x + XN - 1, XN)
    across = lax.rem(x + 2, XN)
    line = [y, y + 1 - 2 * lax.rem(y, 2), lax.rem(y + 2, YN), YN - 1 - y]
    slot_me = lax.rem(me_c, 2) * nb + lax.div(me_c, 2)

    sources = (og_hbm, f_hbm, k_hbm, v_hbm, q_hbm, w_hbm, s_hbm, fwd_hbm, inv_hbm)
    targets = (og_ref, f_ref, k_ref, v_ref, q_ref, w, s_ref, fwd, inv)
    loads = [
        pltpu.make_async_copy(source, target, local_sem.at[i])
        for i, (source, target) in enumerate(zip(sources, targets))
    ]
    for load in loads:
        load.start()

    barrier = pltpu.get_barrier_semaphore()

    def signal(c, t):
        pl.semaphore_signal(barrier, inc=1, device_id=(c, t), device_id_type=MESH)

    signal(me_c, right * YN + y)
    signal(me_c, left * YN + y)
    for j in range(1, YN):
        signal(me_c, x * YN + line[j])

    @pl.loop(1, nctx)
    def _(i):
        signal(lax.rem(me_c + i, nctx), me_t)

    for load in loads[:5]:
        load.wait()
    ft = f_ref[...].astype(F32).T.reshape(nctx, GROUP, rows)
    gated = (k_ref[...].astype(F32) * v_ref[...].astype(F32)).astype(BF16)
    gt = gated.astype(F32).T.reshape(nctx, GROUP, rows)
    fgs[...] = jnp.concatenate([ft, gt], axis=1).astype(BF16)
    qt[...] = q_ref[...].astype(F32).T
    xf[slot_me] = fgs[me_c]

    pl.semaphore_wait(barrier, nctx - 1 + YN + 1)

    def part(ref, h):
        return ref.at[pl.ds(h * half, half), :]

    def send(src, slot, h, dest_x, dest_y, sem):
        pltpu.make_async_remote_copy(
            src_ref=src,
            dst_ref=og_all.at[slot, pl.ds(h * half, half), :],
            send_sem=send_ag,
            recv_sem=sem,
            device_id=(me_c, dest_x * YN + dest_y),
            device_id_type=MESH,
        ).start()

    def arrived(slot, h, sem):
        dst = og_all.at[slot, pl.ds(h * half, half), :]
        pltpu.make_async_copy(dst, dst, sem).wait()

    def send_x(j):
        slot = x * YN + line[j]
        for h in range(2):
            for way, dest in ((h, right if h == 0 else left), (1 - h, left if h == 0 else right)):
                src = part(og_ref, h) if j == 0 else og_all.at[slot, pl.ds(h * half, half), :]
                send(src, slot, h, dest, y, recv_x.at[way, j, h])

    def relay(j):
        for h, source, dest in ((0, left, right), (1, right, left)):
            slot = source * YN + line[j]
            arrived(slot, h, recv_x.at[h, j, h])
            send(og_all.at[slot, pl.ds(h * half, half), :], slot, h, dest, y, recv_r.at[j, h])

    def add(slot, block_value):
        cols = pl.ds(pl.multiple_of(slot * chans, chans), chans)
        acc[...] += lax.dot_general(
            w[:, cols], block_value, (((1,), (1,)), ((), ())), preferred_element_type=F32
        )

    def add_near(j):
        for way, source in ((0, left), (1, right)):
            slot = source * YN + line[j]
            arrived(slot, 1 - way, recv_x.at[way, j, 1 - way])
            add(slot, og_all[slot])

    def add_far(j):
        slot = across * YN + line[j]
        for h in range(2):
            arrived(slot, h, recv_r.at[j, h])
        add(slot, og_all[slot])

    def forward_line(j):
        slot = x * YN + line[j]
        for h in range(2):
            arrived(slot, h, recv_y.at[j - 1, h])
        send_x(j)

    send_x(0)
    for j in range(1, YN):
        for h in range(2):
            send(part(og_ref, h), me_t, h, x, line[j], recv_y.at[j - 1, h])

    def exchange(src, dst, send_sem, recv_sem):
        @pl.loop(1, nctx)
        def _(i):
            peer = lax.rem(me_c + i, nctx)
            pltpu.make_async_remote_copy(
                src_ref=src(peer),
                dst_ref=dst,
                send_sem=send_sem,
                recv_sem=recv_sem,
                device_id=(peer, me_t),
                device_id_type=MESH,
            ).start()

    def drain(ref, count, sem):
        whole = ref.at[pl.ds(0, count)]
        pltpu.make_async_copy(whole, whole, sem).wait()

    exchange(lambda p: fgs.at[p], xf.at[slot_me], send_f, recv_f)

    for load in loads[5:]:
        load.wait()
    acc[...] = lax.dot_general(
        w[:, pl.ds(pl.multiple_of(me_t * chans, chans), chans)], og_ref[...],
        (((1,), (1,)), ((), ())), preferred_element_type=F32,
    )
    for j in range(1, YN):
        forward_line(j)
        relay(j - 1)
        slot = x * YN + line[j]
        add(slot, og_all[slot])
        add_near(j - 1)
        if j >= 2:
            add_far(j - 2)
    relay(YN - 1)
    add_near(YN - 1)
    add_far(YN - 2)
    add_far(YN - 1)

    zs[...] = (acc[...] * qt[...]).reshape(nctx, GROUP, rows)
    exchange(lambda p: zs.at[p], zin.at[slot_me], send_z, recv_z)
    zin[slot_me] = zs[me_c]

    dq_ref[...] = (acc[...].T * s_ref[...].astype(F32)).astype(BF16)
    drain(xf, nctx - 1, recv_f)
    taps = jnp.concatenate(
        [
            xf[pl.ds(0, nb)].reshape(nb * 2 * GROUP, rows),
            xf[pl.ds(nb, nb)].reshape(nb * 2 * GROUP, rows),
        ],
        axis=1,
    )
    both = mm(taps, fwd[...])
    xspec[...] = (both[:, : 2 * block] + both[:, 2 * block :]).reshape(nb, 2 * GROUP, 2 * block)
    lane = lax.broadcasted_iota(jnp.int32, (1, 1, block), 2)
    sign = (1 - 2 * lax.rem(lane, 2)).astype(F32)

    drain(zin, nctx - 1, recv_z)
    signal_in = jnp.concatenate(
        [
            zin[pl.ds(0, nb)].reshape(nb * GROUP, rows),
            zin[pl.ds(nb, nb)].reshape(nb * GROUP, rows),
        ],
        axis=1,
    )
    upper, lower = split(signal_in)
    spec = mm(upper, fwd[...])
    spec = spec[:, : 2 * block] + spec[:, 2 * block :] + mm(lower, fwd[:, : 2 * block])
    spec = spec.reshape(nb, GROUP, 2 * block)
    real, imag = spec[:, :, :block], spec[:, :, block:]
    none = jnp.zeros((1, GROUP, block), F32)
    next_real = jnp.concatenate([real[1:], none], axis=0)
    next_imag = jnp.concatenate([imag[1:], none], axis=0)
    zt[pl.ds(0, nb), :, pl.ds(0, block)] = real + sign * next_imag
    zt[pl.ds(0, nb), :, pl.ds(block, block)] = imag - sign * next_real
    tile = min(4, nb)
    zt[pl.ds(nb, tile)] = jnp.zeros((tile, GROUP, 2 * block), F32)

    width = 128
    for part_of in range(block // width):
        re_cols = pl.ds(part_of * width, width)
        im_cols = pl.ds(block + part_of * width, width)
        for first in range(0, nb, tile):

            def steps(step, sums, re_cols=re_cols, im_cols=im_cols, first=first):
                sums = list(sums)
                for u in range(tile):
                    j = step * tile + u
                    taps_re = xspec[j, :, re_cols]
                    taps_im = xspec[j, :, im_cols]
                    for i in range(tile):
                        z_re = zt[j + first + i, :, re_cols]
                        z_im = zt[j + first + i, :, im_cols]
                        for kind in range(2):
                            a = taps_re[kind * GROUP : (kind + 1) * GROUP]
                            b = taps_im[kind * GROUP : (kind + 1) * GROUP]
                            at = (i * 2 + kind) * 2
                            sums[at] = sums[at] + (a * z_re + b * z_im)
                            sums[at + 1] = sums[at + 1] + (a * z_im - b * z_re)
                return tuple(sums)

            zero = jnp.zeros((GROUP, width), F32)
            sums = lax.fori_loop(0, (nb - first) // tile, steps, (zero,) * (4 * tile))
            for i in range(tile):
                for kind in range(2):
                    at = (i * 2 + kind) * 2
                    lines = pl.ds(kind * GROUP, GROUP)
                    obuf[first + i, lines, re_cols] = sums[at]
                    obuf[first + i, lines, im_cols] = sums[at + 1]

    upper, lower = split(obuf[...].reshape(nb * 2 * GROUP, 2 * block))
    both = mm(upper, inv[...])
    res = both[:, :block] + both[:, block:] + mm(lower, inv[:, :block])
    rs[pl.ds(0, nb)] = res[:, :rows].reshape(nb, 2 * GROUP, rows)
    rs[pl.ds(nb, nb)] = res[:, rows:].reshape(nb, 2 * GROUP, rows)
    exchange(
        lambda p: rs.at[lax.rem(p, 2) * nb + lax.div(p, 2)], ret.at[me_c], send_o, recv_o
    )
    ret[me_c] = rs[slot_me]

    drain(ret, nctx - 1, recv_o)
    du = ret[:, pl.ds(0, GROUP), :].reshape(chans, rows).T
    dk_ref[...] = (du * v_ref[...].astype(F32)).astype(BF16)
    dv_ref[...] = (du * k_ref[...].astype(F32)).astype(BF16)
    lagged = ret[:, pl.ds(GROUP, GROUP), :].reshape(chans, rows).T
    fg_ref[...] = lagged * float(rows * nctx) ** (-0.5)

    drain(og_all, XN * YN - 1, send_ag)
    drain(fgs, nctx - 1, send_f)
    drain(zs, nctx - 1, send_z)
    drain(rs, nctx - 1, send_o)


def body(q_proj, k_proj, v_proj, saved_conv, out_grad, out_weight, filter_taps):
    rows, chans = q_proj.shape
    nctx = lax.axis_size("ctx")
    nb = nctx // 2
    block = 2 * rows
    forward, back = make_tables(block)
    vmem = pl.BlockSpec(memory_space=pltpu.VMEM)
    anywhere = pl.BlockSpec(memory_space=pl.ANY)
    dma = pltpu.SemaphoreType.DMA
    narrow = jax.ShapeDtypeStruct((rows, chans), BF16)
    return pl.pallas_call(
        functools.partial(fused, nctx),
        out_shape=(narrow, narrow, narrow, jax.ShapeDtypeStruct((rows, chans), F32)),
        in_specs=[anywhere] * 9,
        out_specs=(vmem,) * 4,
        scratch_shapes=[pltpu.VMEM((rows, chans), BF16)] * 6
        + [
            pltpu.VMEM(out_weight.shape, BF16),
            pltpu.VMEM(forward.shape, BF16),
            pltpu.VMEM(back.shape, BF16),
            pltpu.VMEM((XN * YN, rows, chans), BF16),
            pltpu.VMEM((chans, rows), F32),
            pltpu.VMEM((chans, rows), F32),
            pltpu.VMEM((nctx, 2 * GROUP, rows), BF16),
            pltpu.VMEM((nctx, 2 * GROUP, rows), BF16),
            pltpu.VMEM((nctx, GROUP, rows), F32),
            pltpu.VMEM((nctx, GROUP, rows), F32),
            pltpu.VMEM((nb, 2 * GROUP, 2 * block), F32),
            pltpu.VMEM((nb + 4, GROUP, 2 * block), F32),
            pltpu.VMEM((nb, 2 * GROUP, 2 * block), F32),
            pltpu.VMEM((nctx, 2 * GROUP, rows), F32),
            pltpu.VMEM((nctx, 2 * GROUP, rows), F32),
            dma((9,)),
            dma,
            dma((YN - 1, 2)),
            dma((2, YN, 2)),
            dma((YN, 2)),
        ]
        + [dma] * 6,
        compiler_params=pltpu.CompilerParams(
            collective_id=0, has_side_effects=True, vmem_limit_bytes=63 * 1024 * 1024
        ),
    )(
        filter_taps, k_proj, v_proj, q_proj, out_grad, saved_conv, out_weight,
        jnp.asarray(forward), jnp.asarray(back),
    )


def solution(mesh):
    block = P("ctx", "tp")
    in_specs = (block, block, block, block, block, P("tp", None), block)
    return jax.shard_map(
        body, mesh=mesh, in_specs=in_specs, out_specs=(block,) * 4, check_vma=False
    )
```

time: 931 us -> 61.3 us (0.07)
  waiting for transfers between devices: 310 us -> 0 us
  starting transfers between devices: 231 us -> 0 us
  matrix products: 181 us -> 0 us
  other arithmetic: 173 us -> 0 us
  Pallas kernels: 0 us -> 54.4 us
  between operations: 13.8 us -> 0.64 us
    ppermute x64 -> x0, starting transfers between devices: 231 us -> none  [the longest x32 164 us: passed_along(): return lax.ppermute(block, axis, route)]
    dot_general x297 -> x0, matrix products: 181 us -> none  [the longest x131 129 us: matmul(): jnp.dot(left, right, precision=lax.Precision.HIGHEST, preferred_element_t...]
    all_gather x2 -> x0, waiting for transfers between devices: 167 us -> none  [the longest x1 97.2 us: body(): whole_filter = lax.all_gather(filter_taps, 'ctx', axis=0, tiled=True)]
    scatter-add x64 -> x0, other arithmetic: 143 us -> none  [the longest x32 72.8 us: add_lags(): filter_terms = filter_terms.at[step].add(lagged[:rows] * active)]
    reduce_scatter x1 -> x0, waiting for transfers between devices: 142 us -> none  [body(): lax.psum_scatter(filter_terms.reshape(blocks * rows, chans), 'ctx', scatt...]
    pallas_call x0 -> x1, Pallas kernels: none -> 54.4 us  [body(): pl.pallas_call(functools.partial(fused, nctx), out_shape=(narrow, narrow,...]
    another operation x32 -> x0, other arithmetic: 25.5 us -> none
  transfers between devices with their start and end apart: 67 -> 0, of which waited for: 3 -> 0; matrix products, arithmetic and copies ran while one was open for 37% -> 0% of each run, Pallas kernels for 0% -> 0%
where the time goes in v1:
time: 61.3 us; the launch traced here: 61 us
  Pallas kernels  54.4 us (89%)
  local copies, waits for them, and re-layouts  5.98 us (10%)
  between operations  0.64 us (1%)
    pallas_call x1, Pallas kernels, body(): pl.pallas_call(functools.partial(fused, nctx), out_shape=(narrow, narrow,...  54.4 us
    unnamed x4, local copies, waits for them, and re-layouts  5.98 us

profile of v1, /device:TPU:1, one launch (start us, length us, event | category | flops | bytes accessed | tf_op | source)
XLA Modules:
  0.0 61.0 jit_solution(6601570066067671863)
XLA Ops:
  0.6 54.4 %shard_map.120 = (bf16[128,256]{1,0:T(8,128)(2,1)}, bf16[128,256]{1,0:T(8,128)(2,1)}, bf16[128,256]{1,0:T(8,128)(2,1)}, f32[128,256]{1,0:T(8,128)}) custom-call(bf16[128,256]{1,0:T(8,128)(2,1)} %f_hbm.1, bf16[128,256]{1,0:T(8,128)(2,1)} %k_hbm.1, bf16[128,256]{1,0:T(8,128)(2,1)} %v_hbm.1, bf16[128,256]{1,0:T(8,128)(2,1)} %q_hbm.1, bf16[128,256]{1,0:T(8,128)(2,1)} %og_hbm.1, ...), custom_call_target="tpu_custom_call" | custom-call | tf_op jit(solution)/shard_map/pallas_call | solution.py:300
  55.1 1.5 %copy.17 = bf16[128,256]{1,0:T(8,128)(2,1)} copy(bf16[128,256]{1,0:T(8,128)(2,1)} %get-tuple-element.8) | data formatting | bytes 131072
  56.5 1.5 %copy.18 = bf16[128,256]{1,0:T(8,128)(2,1)} copy(bf16[128,256]{1,0:T(8,128)(2,1)} %get-tuple-element.9) | data formatting | bytes 131072
  58.0 1.5 %copy.19 = bf16[128,256]{1,0:T(8,128)(2,1)} copy(bf16[128,256]{1,0:T(8,128)(2,1)} %get-tuple-element.10) | data formatting | bytes 131072
  59.5 1.6 %copy.20 = f32[128,256]{1,0:T(8,128)} copy(f32[128,256]{1,0:T(8,128)} %get-tuple-element.11) | data formatting | bytes 262144

commit v2 on v1

--- a/solution.py
+++ b/solution.py
@@ -16,6 +16,7 @@
 XN = 4
 YN = 4
 GROUP = 8
+DIRECT = (0, 3)
 
 
 def halves(table):
@@ -33,6 +34,14 @@
     return halves(forward), halves(back)
 
 
+def far_first(nctx):
+    def hops(i):
+        along = min(i // 4, nctx // 4 - i // 4)
+        return along + (YN if (i // 2) % 2 else 0)
+
+    return sorted(range(1, nctx), key=hops, reverse=True)
+
+
 def split(value):
     upper = value.astype(BF16)
     return upper, (value - upper.astype(F32)).astype(BF16)
@@ -43,10 +52,10 @@
 
 
 def fused(
-    nctx, f_hbm, k_hbm, v_hbm, q_hbm, og_hbm, s_hbm, w_hbm, fwd_hbm, inv_hbm,
-    dq_ref, dk_ref, dv_ref, fg_ref,
-    f_ref, k_ref, v_ref, q_ref, og_ref, s_ref, w, fwd, inv, og_all, acc, qt, fgs, xf, zs, zin, xspec, zt, obuf, rs, ret,
-    local_sem, send_ag, recv_y, recv_x, recv_r, send_f, recv_f, send_z, recv_z, send_o, recv_o,
+    nctx, f_hbm, k_hbm, v_hbm, q_hbm, og_hbm, w_hbm, fwd_hbm, inv_hbm,
+    ret, acc_hbm,
+    f_ref, k_ref, v_ref, q_ref, og_ref, w, fwd, inv, og_all, acc, qt, fgs, xf, zs, zin, xspec, zt, obuf, rs,
+    ready, local_sem, send_ag, recv_y, recv_x, recv_r, send_f, recv_f, send_z, recv_z, send_o, recv_o,
 ):
     rows, chans = q_ref.shape
     nb = nctx // 2
@@ -62,8 +71,8 @@
     line = [y, y + 1 - 2 * lax.rem(y, 2), lax.rem(y + 2, YN), YN - 1 - y]
     slot_me = lax.rem(me_c, 2) * nb + lax.div(me_c, 2)
 
-    sources = (og_hbm, f_hbm, k_hbm, v_hbm, q_hbm, w_hbm, s_hbm, fwd_hbm, inv_hbm)
-    targets = (og_ref, f_ref, k_ref, v_ref, q_ref, w, s_ref, fwd, inv)
+    sources = (og_hbm, f_hbm, k_hbm, v_hbm, q_hbm, w_hbm, fwd_hbm, inv_hbm)
+    targets = (og_ref, f_ref, k_ref, v_ref, q_ref, w, fwd, inv)
     loads = [
         pltpu.make_async_copy(source, target, local_sem.at[i])
         for i, (source, target) in enumerate(zip(sources, targets))
@@ -76,25 +85,28 @@
     def signal(c, t):
         pl.semaphore_signal(barrier, inc=1, device_id=(c, t), device_id_type=MESH)
 
-    signal(me_c, right * YN + y)
-    signal(me_c, left * YN + y)
+    core = me_c + 1 - 2 * lax.rem(me_c, 2)
+    turn = 2 - 4 * lax.rem(lax.div(me_c, 2), 2)
+    chip_set = (core, me_c + turn, core + turn)
+
+    def around(steps):
+        return [lax.rem(me_c + i, nctx) for i in sorted({steps % nctx, -steps % nctx} - {0})]
+
+    for t in (right, left, across):
+        signal(me_c, t * YN + y)
     for j in range(1, YN):
         signal(me_c, x * YN + line[j])
-
-    @pl.loop(1, nctx)
-    def _(i):
-        signal(lax.rem(me_c + i, nctx), me_t)
-
-    for load in loads[:5]:
-        load.wait()
-    ft = f_ref[...].astype(F32).T.reshape(nctx, GROUP, rows)
-    gated = (k_ref[...].astype(F32) * v_ref[...].astype(F32)).astype(BF16)
-    gt = gated.astype(F32).T.reshape(nctx, GROUP, rows)
-    fgs[...] = jnp.concatenate([ft, gt], axis=1).astype(BF16)
-    qt[...] = q_ref[...].astype(F32).T
-    xf[slot_me] = fgs[me_c]
-
-    pl.semaphore_wait(barrier, nctx - 1 + YN + 1)
+    near = (*around(4), *chip_set)
+    for c in near:
+        signal(c, me_t)
+
+    def tell(partners, sem):
+        for c in partners:
+            pl.semaphore_signal(sem, inc=1, device_id=(c, me_t), device_id_type=MESH)
+
+    loads[0].wait()
+    pl.semaphore_wait(barrier, 3 + YN - 1 + len(near))
+    tell(chip_set, ready.at[0])
 
     def part(ref, h):
         return ref.at[pl.ds(h * half, half), :]
@@ -113,17 +125,21 @@
         dst = og_all.at[slot, pl.ds(h * half, half), :]
         pltpu.make_async_copy(dst, dst, sem).wait()
 
-    def send_x(j):
+    def send_x(j, h):
         slot = x * YN + line[j]
-        for h in range(2):
-            for way, dest in ((h, right if h == 0 else left), (1 - h, left if h == 0 else right)):
-                src = part(og_ref, h) if j == 0 else og_all.at[slot, pl.ds(h * half, half), :]
-                send(src, slot, h, dest, y, recv_x.at[way, j, h])
+        src = part(og_ref, h) if j == 0 else og_all.at[slot, pl.ds(h * half, half), :]
+        if j in DIRECT:
+            send(src, slot, h, across, y, recv_r.at[j, h])
+        first, second = (right, left) if h == 0 else (left, right)
+        send(src, slot, h, first, y, recv_x.at[h, j, h])
+        send(src, slot, h, second, y, recv_x.at[1 - h, j, h])
 
     def relay(j):
         for h, source, dest in ((0, left, right), (1, right, left)):
             slot = source * YN + line[j]
             arrived(slot, h, recv_x.at[h, j, h])
+            if j in DIRECT:
+                continue
             send(og_all.at[slot, pl.ds(h * half, half), :], slot, h, dest, y, recv_r.at[j, h])
 
     def add(slot, block_value):
@@ -148,16 +164,15 @@
         slot = x * YN + line[j]
         for h in range(2):
             arrived(slot, h, recv_y.at[j - 1, h])
-        send_x(j)
-
-    send_x(0)
-    for j in range(1, YN):
-        for h in range(2):
+            send_x(j, h)
+
+    for h in range(2):
+        for j in range(1, YN):
             send(part(og_ref, h), me_t, h, x, line[j], recv_y.at[j - 1, h])
+        send_x(0, h)
 
     def exchange(src, dst, send_sem, recv_sem):
-        @pl.loop(1, nctx)
-        def _(i):
+        for i in far_first(nctx):
             peer = lax.rem(me_c + i, nctx)
             pltpu.make_async_remote_copy(
                 src_ref=src(peer),
@@ -172,7 +187,14 @@
         whole = ref.at[pl.ds(0, count)]
         pltpu.make_async_copy(whole, whole, sem).wait()
 
-    exchange(lambda p: fgs.at[p], xf.at[slot_me], send_f, recv_f)
+    for load in loads[1:5]:
+        load.wait()
+    ft = f_ref[...].astype(F32).T.reshape(nctx, GROUP, rows)
+    gated = (k_ref[...].astype(F32) * v_ref[...].astype(F32)).astype(BF16)
+    gt = gated.astype(F32).T.reshape(nctx, GROUP, rows)
+    fgs[...] = jnp.concatenate([ft, gt], axis=1).astype(BF16)
+    qt[...] = q_ref[...].astype(F32).T
+    xf[slot_me] = fgs[me_c]
 
     for load in loads[5:]:
         load.wait()
@@ -180,9 +202,15 @@
         w[:, pl.ds(pl.multiple_of(me_t * chans, chans), chans)], og_ref[...],
         (((1,), (1,)), ((), ())), preferred_element_type=F32,
     )
+    rounds = (chip_set, around(4), around(8))
     for j in range(1, YN):
         forward_line(j)
         relay(j - 1)
+        pl.semaphore_wait(ready.at[j - 1], len(rounds[j - 1]))
+        if j < 3:
+            tell(rounds[j], ready.at[j])
+        else:
+            exchange(lambda p: fgs.at[p], xf.at[slot_me], send_f, recv_f)
         slot = x * YN + line[j]
         add(slot, og_all[slot])
         add_near(j - 1)
@@ -197,7 +225,8 @@
     exchange(lambda p: zs.at[p], zin.at[slot_me], send_z, recv_z)
     zin[slot_me] = zs[me_c]
 
-    dq_ref[...] = (acc[...].T * s_ref[...].astype(F32)).astype(BF16)
+    save = pltpu.make_async_copy(acc, acc_hbm, local_sem.at[8])
+    save.start()
     drain(xf, nctx - 1, recv_f)
     taps = jnp.concatenate(
         [
@@ -272,19 +301,53 @@
     exchange(
         lambda p: rs.at[lax.rem(p, 2) * nb + lax.div(p, 2)], ret.at[me_c], send_o, recv_o
     )
-    ret[me_c] = rs[slot_me]
-
+    own = pltpu.make_async_copy(rs.at[slot_me], ret.at[me_c], local_sem.at[9])
+    own.start()
     drain(ret, nctx - 1, recv_o)
-    du = ret[:, pl.ds(0, GROUP), :].reshape(chans, rows).T
-    dk_ref[...] = (du * v_ref[...].astype(F32)).astype(BF16)
-    dv_ref[...] = (du * k_ref[...].astype(F32)).astype(BF16)
-    lagged = ret[:, pl.ds(GROUP, GROUP), :].reshape(chans, rows).T
-    fg_ref[...] = lagged * float(rows * nctx) ** (-0.5)
-
+    own.wait()
+    save.wait()
     drain(og_all, XN * YN - 1, send_ag)
     drain(fgs, nctx - 1, send_f)
     drain(zs, nctx - 1, send_z)
     drain(rs, nctx - 1, send_o)
+
+
+def finish(
+    ret_hbm, acc_hbm, s_hbm, k_hbm, v_hbm, dq_hbm, dk_hbm, dv_hbm, fg_hbm,
+    ret, acc, s_ref, k_ref, v_ref, dq, dk, dv, fg, sem_in, sem_out,
+):
+    rows, chans = s_ref.shape
+    loads = [
+        pltpu.make_async_copy(source, target, sem_in.at[i])
+        for i, (source, target) in enumerate(
+            ((acc_hbm, acc), (s_hbm, s_ref), (ret_hbm, ret), (k_hbm, k_ref), (v_hbm, v_ref))
+        )
+    ]
+    for load in loads:
+        load.start()
+    stores = [
+        pltpu.make_async_copy(source, target, sem_out.at[i])
+        for i, (source, target) in enumerate(
+            ((dq, dq_hbm), (dk, dk_hbm), (dv, dv_hbm), (fg, fg_hbm))
+        )
+    ]
+    loads[0].wait()
+    loads[1].wait()
+    dq[...] = (acc[...].T * s_ref[...].astype(F32)).astype(BF16)
+    stores[0].start()
+    loads[2].wait()
+    lagged = ret[:, pl.ds(GROUP, GROUP), :].reshape(chans, rows).T
+    fg[...] = lagged * float(rows * ret.shape[0]) ** (-0.5)
+    stores[3].start()
+    du = ret[:, pl.ds(0, GROUP), :].reshape(chans, rows).T
+    loads[3].wait()
+    loads[4].wait()
+    dk[...] = (du * v_ref[...].astype(F32)).astype(BF16)
+    stores[1].start()
+    dv[...] = (du * k_ref[...].astype(F32)).astype(BF16)
+    stores[2].start()
+    for store in stores:
+        store.wait()
 
 
 def body(q_proj, k_proj, v_proj, saved_conv, out_grad, out_weight, filter_taps):
@@ -293,16 +356,19 @@
     nb = nctx // 2
     block = 2 * rows
     forward, back = make_tables(block)
-    vmem = pl.BlockSpec(memory_space=pltpu.VMEM)
-    anywhere = pl.BlockSpec(memory_space=pl.ANY)
+    hbm = pl.BlockSpec(memory_space=pltpu.HBM)
     dma = pltpu.SemaphoreType.DMA
     narrow = jax.ShapeDtypeStruct((rows, chans), BF16)
-    return pl.pallas_call(
+    shapes = (narrow, narrow, narrow, jax.ShapeDtypeStruct((rows, chans), F32))
+    results = pl.pallas_call(
         functools.partial(fused, nctx),
-        out_shape=(narrow, narrow, narrow, jax.ShapeDtypeStruct((rows, chans), F32)),
-        in_specs=[anywhere] * 9,
-        out_specs=(vmem,) * 4,
-        scratch_shapes=[pltpu.VMEM((rows, chans), BF16)] * 6
+        out_shape=(
+            jax.ShapeDtypeStruct((nctx, 2 * GROUP, rows), F32),
+            jax.ShapeDtypeStruct((chans, rows), F32),
+        ),
+        in_specs=[hbm] * 8,
+        out_specs=(hbm,) * 2,
+        scratch_shapes=[pltpu.VMEM((rows, chans), BF16)] * 5
         + [
             pltpu.VMEM(out_weight.shape, BF16),
             pltpu.VMEM(forward.shape, BF16),
@@ -318,8 +384,8 @@
             pltpu.VMEM((nb + 4, GROUP, 2 * block), F32),
             pltpu.VMEM((nb, 2 * GROUP, 2 * block), F32),
             pltpu.VMEM((nctx, 2 * GROUP, rows), F32),
-            pltpu.VMEM((nctx, 2 * GROUP, rows), F32),
-            dma((9,)),
+            pltpu.SemaphoreType.REGULAR((3,)),
+            dma((10,)),
             dma,
             dma((YN - 1, 2)),
             dma((2, YN, 2)),
@@ -330,9 +396,22 @@
             collective_id=0, has_side_effects=True, vmem_limit_bytes=63 * 1024 * 1024
         ),
     )(
-        filter_taps, k_proj, v_proj, q_proj, out_grad, saved_conv, out_weight,
+        filter_taps, k_proj, v_proj, q_proj, out_grad, out_weight,
         jnp.asarray(forward), jnp.asarray(back),
     )
+    return pl.pallas_call(
+        finish,
+        out_shape=shapes,
+        in_specs=[hbm] * 5,
+        out_specs=(hbm,) * 4,
+        scratch_shapes=[
+            pltpu.VMEM((nctx, 2 * GROUP, rows), F32),
+            pltpu.VMEM((chans, rows), F32),
+        ]
+        + [pltpu.VMEM((rows, chans), BF16)] * 6
+        + [pltpu.VMEM((rows, chans), F32), dma((5,)), dma((4,))],
+        compiler_params=pltpu.CompilerParams(vmem_limit_bytes=63 * 1024 * 1024),
+    )(*results, saved_conv, k_proj, v_proj)
 
 
 def solution(mesh):

time: 61.3 us -> 51.5 us (0.84)
  local copies, waits for them, and re-layouts: 5.98 us -> 0 us
  Pallas kernels: 54.4 us -> 50.7 us
    unnamed x4 -> x0, local copies, waits for them, and re-layouts: 5.98 us -> none
    pallas_call x1 -> x2, Pallas kernels: 54.4 us -> 50.7 us  [the longest x1 48.7 us: body(): pl.pallas_call(functools.partial(fused, nctx), out_shape=(jax.ShapeDtypeS...]
where the time goes in v2:
time: 51.5 us; the launch traced here: 51.3 us
  Pallas kernels  50.7 us (98%)
  between operations  0.64 us (1%)
    pallas_call x1, Pallas kernels, body(): pl.pallas_call(functools.partial(fused, nctx), out_shape=(jax.ShapeDtypeS...  48.7 us
    pallas_call x1, Pallas kernels, body(): pl.pallas_call(finish, out_shape=shapes, in_specs=[hbm] * 5, out_specs=(h...  1.94 us

profile of v2, /device:TPU:1, one launch (start us, length us, event | category | flops | bytes accessed | tf_op | source)
XLA Modules:
  0.0 51.3 jit_solution(10199011420282202421)
XLA Ops:
  0.6 48.7 %shard_map.120 = (f32[32,16,128]{2,1,0:T(8,128)}, f32[256,128]{1,0:T(8,128)}) custom-call(bf16[128,256]{1,0:T(8,128)(2,1)} %f_hbm.1, bf16[128,256]{1,0:T(8,128)(2,1)} %k_hbm.3, bf16[128,256]{1,0:T(8,128)(2,1)} %v_hbm.3, bf16[128,256]{1,0:T(8,128)(2,1)} %q_hbm.1, bf16[128,256]{1,0:T(8,128)(2,1)} %og_hbm.1, bf16[256,4096]{1,0:T(8,128)(2,1)} %w_hbm.1, ...), custom_call_target="tpu_custom_call" | custom-call | tf_op jit(solution)/shard_map/pallas_call | solution.py:363
  49.4 1.9 %shard_map.121 = (bf16[128,256]{1,0:T(8,128)(2,1)}, bf16[128,256]{1,0:T(8,128)(2,1)}, bf16[128,256]{1,0:T(8,128)(2,1)}, f32[128,256]{1,0:T(8,128)}) custom-call(f32[32,16,128]{2,1,0:T(8,128)} %get-tuple-element.6.ret_hbm, f32[256,128]{1,0:T(8,128)} %get-tuple-element.7.acc_hbm, bf16[128,256]{1,0:T(8,128)(2,1)} %s_hbm.1, bf16[128,256]{1,0:T(8,128)(2,1)} %k_hbm.3, ...), custom_call_target="tpu_custom_call" | custom-call | tf_op jit(solution)/shard_map/pallas_call | solution.py:402

commit v3 on v2

--- a/solution.py
+++ b/solution.py
@@ -36,10 +36,9 @@
 
 def far_first(nctx):
     def hops(i):
-        along = min(i // 4, nctx // 4 - i // 4)
-        return along + (YN if (i // 2) % 2 else 0)
-
-    return sorted(range(1, nctx), key=hops, reverse=True)
+        return min(i // 4, nctx // 4 - i // 4)
+
+    return sorted(range(nctx), key=hops, reverse=True)
 
 
 def split(value):
@@ -85,9 +84,9 @@
     def signal(c, t):
         pl.semaphore_signal(barrier, inc=1, device_id=(c, t), device_id_type=MESH)
 
+    mate = x * YN + lax.rem(y + 2, YN)
     core = me_c + 1 - 2 * lax.rem(me_c, 2)
     turn = 2 - 4 * lax.rem(lax.div(me_c, 2), 2)
-    chip_set = (core, me_c + turn, core + turn)
 
     def around(steps):
         return [lax.rem(me_c + i, nctx) for i in sorted({steps % nctx, -steps % nctx} - {0})]
@@ -96,7 +95,9 @@
         signal(me_c, t * YN + y)
     for j in range(1, YN):
         signal(me_c, x * YN + line[j])
-    near = (*around(4), *chip_set)
+    for c in (core, me_c + turn, core + turn):
+        signal(c, mate)
+    near = (*around(4), *around(8))
     for c in near:
         signal(c, me_t)
 
@@ -105,8 +106,8 @@
             pl.semaphore_signal(sem, inc=1, device_id=(c, me_t), device_id_type=MESH)
 
     loads[0].wait()
-    pl.semaphore_wait(barrier, 3 + YN - 1 + len(near))
-    tell(chip_set, ready.at[0])
+    pl.semaphore_wait(barrier, 6 + YN - 1 + len(near))
+    tell(around(4), ready.at[0])
 
     def part(ref, h):
         return ref.at[pl.ds(h * half, half), :]
@@ -179,7 +180,7 @@
                 dst_ref=dst,
                 send_sem=send_sem,
                 recv_sem=recv_sem,
-                device_id=(peer, me_t),
+                device_id=(peer, mate),
                 device_id_type=MESH,
             ).start()
 
@@ -194,7 +195,6 @@
     gt = gated.astype(F32).T.reshape(nctx, GROUP, rows)
     fgs[...] = jnp.concatenate([ft, gt], axis=1).astype(BF16)
     qt[...] = q_ref[...].astype(F32).T
-    xf[slot_me] = fgs[me_c]
 
     for load in loads[5:]:
         load.wait()
@@ -202,14 +202,15 @@
         w[:, pl.ds(pl.multiple_of(me_t * chans, chans), chans)], og_ref[...],
         (((1,), (1,)), ((), ())), preferred_element_type=F32,
     )
-    rounds = (chip_set, around(4), around(8))
+    rounds = (around(4), around(12))
     for j in range(1, YN):
         forward_line(j)
         relay(j - 1)
-        pl.semaphore_wait(ready.at[j - 1], len(rounds[j - 1]))
         if j < 3:
-            tell(rounds[j], ready.at[j])
-        else:
+            pl.semaphore_wait(ready.at[j - 1], len(rounds[j - 1]))
+        if j == 1:
+            tell(rounds[1], ready.at[1])
+        if j == 3:
             exchange(lambda p: fgs.at[p], xf.at[slot_me], send_f, recv_f)
         slot = x * YN + line[j]
         add(slot, og_all[slot])
@@ -223,11 +224,10 @@
 
     zs[...] = (acc[...] * qt[...]).reshape(nctx, GROUP, rows)
     exchange(lambda p: zs.at[p], zin.at[slot_me], send_z, recv_z)
-    zin[slot_me] = zs[me_c]
 
     save = pltpu.make_async_copy(acc, acc_hbm, local_sem.at[8])
     save.start()
-    drain(xf, nctx - 1, recv_f)
+    drain(xf, nctx, recv_f)
     taps = jnp.concatenate(
         [
             xf[pl.ds(0, nb)].reshape(nb * 2 * GROUP, rows),
@@ -240,7 +240,7 @@
     lane = lax.broadcasted_iota(jnp.int32, (1, 1, block), 2)
     sign = (1 - 2 * lax.rem(lane, 2)).astype(F32)
 
-    drain(zin, nctx - 1, recv_z)
+    drain(zin, nctx, recv_z)
     signal_in = jnp.concatenate(
         [
             zin[pl.ds(0, nb)].reshape(nb * GROUP, rows),
@@ -296,20 +296,18 @@
     upper, lower = split(obuf[...].reshape(nb * 2 * GROUP, 2 * block))
     both = mm(upper, inv[...])
     res = both[:, :block] + both[:, block:] + mm(lower, inv[:, :block])
-    rs[pl.ds(0, nb)] = res[:, :rows].reshape(nb, 2 * GROUP, rows)
-    rs[pl.ds(nb, nb)] = res[:, rows:].reshape(nb, 2 * GROUP, rows)
+    coded = (res * jnp.abs(res)).astype(BF16)
+    rs[pl.ds(0, nb)] = coded[:, :rows].reshape(nb, 2 * GROUP, rows)
+    rs[pl.ds(nb, nb)] = coded[:, rows:].reshape(nb, 2 * GROUP, rows)
     exchange(
         lambda p: rs.at[lax.rem(p, 2) * nb + lax.div(p, 2)], ret.at[me_c], send_o, recv_o
     )
-    own = pltpu.make_async_copy(rs.at[slot_me], ret.at[me_c], local_sem.at[9])
-    own.start()
-    drain(ret, nctx - 1, recv_o)
-    own.wait()
+    drain(ret, nctx, recv_o)
     save.wait()
     drain(og_all, XN * YN - 1, send_ag)
-    drain(fgs, nctx - 1, send_f)
-    drain(zs, nctx - 1, send_z)
-    drain(rs, nctx - 1, send_o)
+    drain(fgs, nctx, send_f)
+    drain(zs, nctx, send_z)
+    drain(rs, nctx, send_o)
 
 
 def finish(
@@ -336,10 +334,13 @@
     dq[...] = (acc[...].T * s_ref[...].astype(F32)).astype(BF16)
     stores[0].start()
     loads[2].wait()
-    lagged = ret[:, pl.ds(GROUP, GROUP), :].reshape(chans, rows).T
+    coded = ret[...].astype(F32)
+    root = jnp.sqrt(jnp.abs(coded))
+    plain = jnp.where(coded < 0.0, -root, root)
+    lagged = plain[:, GROUP:, :].reshape(chans, rows).T
     fg[...] = lagged * float(rows * ret.shape[0]) ** (-0.5)
     stores[3].start()
-    du = ret[:, pl.ds(0, GROUP), :].reshape(chans, rows).T
+    du = plain[:, :GROUP, :].reshape(chans, rows).T
     loads[3].wait()
     loads[4].wait()
     dk[...] = (du * v_ref[...].astype(F32)).astype(BF16)
@@ -363,7 +364,7 @@
     results = pl.pallas_call(
         functools.partial(fused, nctx),
         out_shape=(
-            jax.ShapeDtypeStruct((nctx, 2 * GROUP, rows), F32),
+            jax.ShapeDtypeStruct((nctx, 2 * GROUP, rows), BF16),
             jax.ShapeDtypeStruct((chans, rows), F32),
         ),
         in_specs=[hbm] * 8,
@@ -383,9 +384,9 @@
             pltpu.VMEM((nb, 2 * GROUP, 2 * block), F32),
             pltpu.VMEM((nb + 4, GROUP, 2 * block), F32),
             pltpu.VMEM((nb, 2 * GROUP, 2 * block), F32),
-            pltpu.VMEM((nctx, 2 * GROUP, rows), F32),
-            pltpu.SemaphoreType.REGULAR((3,)),
-            dma((10,)),
+            pltpu.VMEM((nctx, 2 * GROUP, rows), BF16),
+            pltpu.SemaphoreType.REGULAR((2,)),
+            dma((9,)),
             dma,
             dma((YN - 1, 2)),
             dma((2, YN, 2)),
@@ -405,7 +406,7 @@
         in_specs=[hbm] * 5,
         out_specs=(hbm,) * 4,
         scratch_shapes=[
-            pltpu.VMEM((nctx, 2 * GROUP, rows), F32),
+            pltpu.VMEM((nctx, 2 * GROUP, rows), BF16),
             pltpu.VMEM((chans, rows), F32),
         ]
         + [pltpu.VMEM((rows, chans), BF16)] * 6

time: 51.5 us -> 46.5 us (0.903)
  Pallas kernels: 50.7 us -> 45.7 us
    pallas_call x1, Pallas kernels: 48.7 us -> 43.8 us  [body(): pl.pallas_call(functools.partial(fused, nctx), out_shape=(jax.ShapeDtypeS...]
where the time goes in v3:
time: 46.5 us; the launch traced here: 46.3 us
  Pallas kernels  45.7 us (98%)
  between operations  0.64 us (1%)
    pallas_call x1, Pallas kernels, body(): pl.pallas_call(functools.partial(fused, nctx), out_shape=(jax.ShapeDtypeS...  43.8 us
    pallas_call x1, Pallas kernels, body(): pl.pallas_call(finish, out_shape=shapes, in_specs=[hbm] * 5, out_specs=(h...  1.93 us

profile of v3, /device:TPU:1, one launch (start us, length us, event | category | flops | bytes accessed | tf_op | source)
XLA Modules:
  0.0 46.3 jit_solution(14438186555090018800)
XLA Ops:
  0.6 43.8 %shard_map.120 = (bf16[32,16,128]{2,1,0:T(8,128)(2,1)}, f32[256,128]{1,0:T(8,128)}) custom-call(bf16[128,256]{1,0:T(8,128)(2,1)} %f_hbm.1, bf16[128,256]{1,0:T(8,128)(2,1)} %k_hbm.3, bf16[128,256]{1,0:T(8,128)(2,1)} %v_hbm.3, bf16[128,256]{1,0:T(8,128)(2,1)} %q_hbm.1, bf16[128,256]{1,0:T(8,128)(2,1)} %og_hbm.1, bf16[256,4096]{1,0:T(8,128)(2,1)} %w_hbm.1, ...), custom_call_target="tpu_custom_call" | custom-call | tf_op jit(solution)/shard_map/pallas_call | solution.py:364
  44.4 1.9 %shard_map.121 = (bf16[128,256]{1,0:T(8,128)(2,1)}, bf16[128,256]{1,0:T(8,128)(2,1)}, bf16[128,256]{1,0:T(8,128)(2,1)}, f32[128,256]{1,0:T(8,128)}) custom-call(bf16[32,16,128]{2,1,0:T(8,128)(2,1)} %get-tuple-element.6.ret_hbm, f32[256,128]{1,0:T(8,128)} %get-tuple-element.7.acc_hbm, bf16[128,256]{1,0:T(8,128)(2,1)} %s_hbm.1, bf16[128,256]{1,0:T(8,128)(2,1)} %k_hbm.3, ...), custom_call_target="tpu_custom_call" | custom-call | tf_op jit(solution)/shard_map/pallas_call | solution.py:403

commit v4 on v3

--- a/solution.py
+++ b/solution.py
@@ -34,11 +34,29 @@
     return halves(forward), halves(back)
 
 
-def far_first(nctx):
-    def hops(i):
-        return min(i // 4, nctx // 4 - i // 4)
-
-    return sorted(range(nctx), key=hops, reverse=True)
+def planes(nctx):
+    return nctx // 4
+
+
+def ways_in(nctx):
+    count = planes(nctx)
+
+    def hops(one, other):
+        return min((one - other) % count, (other - one) % count)
+
+    return sorted(
+        range(nctx), key=lambda c: hops(c // 4, count - 1) + hops(c // 4, 0), reverse=True
+    )
+
+
+def ways_out(nctx):
+    count = planes(nctx)
+
+    def entry(c):
+        z = c // 4
+        return z + (2 if 2 * z >= count else 0) + (4 if (c // 2) % 2 else 0)
+
+    return sorted(range(nctx), key=entry)
 
 
 def split(value):
@@ -167,14 +185,14 @@
             arrived(slot, h, recv_y.at[j - 1, h])
             send_x(j, h)
 
+    for j in range(1, YN):
+        for h in range(2):
+            send(part(og_ref, h), me_t, h, x, line[j], recv_y.at[j - 1, h])
     for h in range(2):
-        for j in range(1, YN):
-            send(part(og_ref, h), me_t, h, x, line[j], recv_y.at[j - 1, h])
         send_x(0, h)
 
-    def exchange(src, dst, send_sem, recv_sem):
-        for i in far_first(nctx):
-            peer = lax.rem(me_c + i, nctx)
+    def exchange(order, src, dst, send_sem, recv_sem):
+        for peer in order:
             pltpu.make_async_remote_copy(
                 src_ref=src(peer),
                 dst_ref=dst,
@@ -203,15 +221,14 @@
         (((1,), (1,)), ((), ())), preferred_element_type=F32,
     )
     rounds = (around(4), around(12))
+    pl.semaphore_wait(ready.at[0], len(rounds[0]))
+    tell(rounds[1], ready.at[1])
     for j in range(1, YN):
         forward_line(j)
         relay(j - 1)
-        if j < 3:
-            pl.semaphore_wait(ready.at[j - 1], len(rounds[j - 1]))
-        if j == 1:
-            tell(rounds[1], ready.at[1])
-        if j == 3:
-            exchange(lambda p: fgs.at[p], xf.at[slot_me], send_f, recv_f)
+        if j == 2:
+            pl.semaphore_wait(ready.at[1], len(rounds[1]))
+            exchange(ways_in(nctx), lambda p: fgs.at[p], xf.at[slot_me], send_f, recv_f)
         slot = x * YN + line[j]
         add(slot, og_all[slot])
         add_near(j - 1)
@@ -223,7 +240,7 @@
     add_far(YN - 1)
 
     zs[...] = (acc[...] * qt[...]).reshape(nctx, GROUP, rows)
-    exchange(lambda p: zs.at[p], zin.at[slot_me], send_z, recv_z)
+    exchange(ways_in(nctx), lambda p: zs.at[p], zin.at[slot_me], send_z, recv_z)
 
     save = pltpu.make_async_copy(acc, acc_hbm, local_sem.at[8])
     save.start()
@@ -262,10 +279,10 @@
     zt[pl.ds(nb, tile)] = jnp.zeros((tile, GROUP, 2 * block), F32)
 
     width = 128
-    for part_of in range(block // width):
-        re_cols = pl.ds(part_of * width, width)
-        im_cols = pl.ds(block + part_of * width, width)
-        for first in range(0, nb, tile):
+    for first in range(0, nb, tile):
+        for part_of in range(block // width):
+            re_cols = pl.ds(part_of * width, width)
+            im_cols = pl.ds(block + part_of * width, width)
 
             def steps(step, sums, re_cols=re_cols, im_cols=im_cols, first=first):
                 sums = list(sums)
@@ -292,16 +309,17 @@
                     lines = pl.ds(kind * GROUP, GROUP)
                     obuf[first + i, lines, re_cols] = sums[at]
                     obuf[first + i, lines, im_cols] = sums[at + 1]
-
-    upper, lower = split(obuf[...].reshape(nb * 2 * GROUP, 2 * block))
-    both = mm(upper, inv[...])
-    res = both[:, :block] + both[:, block:] + mm(lower, inv[:, :block])
-    coded = (res * jnp.abs(res)).astype(BF16)
-    rs[pl.ds(0, nb)] = coded[:, :rows].reshape(nb, 2 * GROUP, rows)
-    rs[pl.ds(nb, nb)] = coded[:, rows:].reshape(nb, 2 * GROUP, rows)
-    exchange(
-        lambda p: rs.at[lax.rem(p, 2) * nb + lax.div(p, 2)], ret.at[me_c], send_o, recv_o
-    )
+        upper, lower = split(obuf[pl.ds(first, tile)].reshape(tile * 2 * GROUP, 2 * block))
+        both = mm(upper, inv[...])
+        res = both[:, :block] + both[:, block:] + mm(lower, inv[:, :block])
+        coded = (res * jnp.abs(res)).astype(BF16)
+        rs[pl.ds(first, tile)] = coded[:, :rows].reshape(tile, 2 * GROUP, rows)
+        rs[pl.ds(nb + first, tile)] = coded[:, rows:].reshape(tile, 2 * GROUP, rows)
+        exchange(
+            [c for c in ways_out(nctx) if first <= c // 2 < first + tile],
+            lambda p: rs.at[p % 2 * nb + p // 2], ret.at[me_c], send_o, recv_o,
+        )
+
     drain(ret, nctx, recv_o)
     save.wait()
     drain(og_all, XN * YN - 1, send_ag)

time: 46.5 us -> 45.1 us (0.970)
  Pallas kernels: 45.7 us -> 44.3 us
    pallas_call x1, Pallas kernels: 43.8 us -> 42.3 us  [body(): pl.pallas_call(functools.partial(fused, nctx), out_shape=(jax.ShapeDtypeS...]
where the time goes in v4:
time: 45.1 us; the launch traced here: 44.9 us
  Pallas kernels  44.3 us (98%)
  between operations  0.64 us (1%)
    pallas_call x1, Pallas kernels, body(): pl.pallas_call(functools.partial(fused, nctx), out_shape=(jax.ShapeDtypeS...  42.3 us
    pallas_call x1, Pallas kernels, body(): pl.pallas_call(finish, out_shape=shapes, in_specs=[hbm] * 5, out_specs=(h...  1.93 us

profile of v4, /device:TPU:1, one launch (start us, length us, event | category | flops | bytes accessed | tf_op | source)
XLA Modules:
  0.0 44.9 jit_solution(16695817626158974149)
XLA Ops:
  0.6 42.3 %shard_map.120 = (bf16[32,16,128]{2,1,0:T(8,128)(2,1)}, f32[256,128]{1,0:T(8,128)}) custom-call(bf16[128,256]{1,0:T(8,128)(2,1)} %f_hbm.1, bf16[128,256]{1,0:T(8,128)(2,1)} %k_hbm.3, bf16[128,256]{1,0:T(8,128)(2,1)} %v_hbm.3, bf16[128,256]{1,0:T(8,128)(2,1)} %q_hbm.1, bf16[128,256]{1,0:T(8,128)(2,1)} %og_hbm.1, bf16[256,4096]{1,0:T(8,128)(2,1)} %w_hbm.1, ...), custom_call_target="tpu_custom_call" | custom-call | tf_op jit(solution)/shard_map/pallas_call | solution.py:382
  43.0 1.9 %shard_map.121 = (bf16[128,256]{1,0:T(8,128)(2,1)}, bf16[128,256]{1,0:T(8,128)(2,1)}, bf16[128,256]{1,0:T(8,128)(2,1)}, f32[128,256]{1,0:T(8,128)}) custom-call(bf16[32,16,128]{2,1,0:T(8,128)(2,1)} %get-tuple-element.6.ret_hbm, f32[256,128]{1,0:T(8,128)} %get-tuple-element.7.acc_hbm, bf16[128,256]{1,0:T(8,128)(2,1)} %s_hbm.1, bf16[128,256]{1,0:T(8,128)(2,1)} %k_hbm.3, ...), custom_call_target="tpu_custom_call" | custom-call | tf_op jit(solution)/shard_map/pallas_call | solution.py:421
